TPU v7x, 32 devices: a whole 2x2x4 slice. The times are simulated.
32 devices in a mesh: row: 4 (over y, x), col: 8 (over z, core).
Axes of the slice: x: 2, y: 2, z: 4, core: 2. Of those that a mesh axis runs over, the one named last changes fastest.
Arguments:
- fingerprints: bfloat16 [8192, 1024], P(('row', 'col')), as said below
- probes: bfloat16 [8192, 256], P(('row', 'col')), may hold values from -6 to 6
Outputs:
- image: float32 [8192, 256], P(('row', 'col'))
Inputs may be any that keep to these rules, and one draw needn't show every extreme that they name: `fingerprints`: every entry is positive.
All inputs are finite; a program needn't handle non-finite values.
Results may differ from a plain program's by a relative error of at most 0.0031.
Values may be sent and summed in bfloat16 or wider, within the bound.
A program may use at most 64 MiB of HBM per device.

v0:
```python
import math
import jax
import jax.numpy as jnp
from jax import lax
from jax.sharding import PartitionSpec as P


def squares(rows_now):
    values = rows_now.astype(jnp.float32)
    return jnp.sum(values * values, axis=1)


def tanimoto(first_rows, second_rows, first_sq, second_sq):
    inner = lax.dot_general(
        first_rows, second_rows, (((1,), (1,)), ((), ())), preferred_element_type=jnp.float32
    )
    kernel = inner / (first_sq[:, None] + second_sq[None, :] - inner)
    return kernel.astype(jnp.bfloat16)


def per_device(fingerprints, probes):
    molecules = fingerprints.shape[0] * lax.axis_size("row") * lax.axis_size("col")
    factor = 1.0 / math.sqrt(molecules)
    column_rows, column_probes = (
        lax.all_gather(fingerprints, "row", axis=0, tiled=True),
        lax.all_gather(probes, "row", axis=0, tiled=True),
    )
    column_sq = squares(column_rows)
    shard_rows = lax.all_gather(fingerprints, "col", axis=0, tiled=True)
    kernel = tanimoto(shard_rows, column_rows, squares(shard_rows), column_sq)
    partial_value = jnp.dot(kernel, column_probes, preferred_element_type=jnp.float32)
    owned = lax.psum_scatter(partial_value, "col", scatter_dimension=0, tiled=True)
    return owned * factor


def solution(mesh):
    return jax.shard_map(
        per_device,
        mesh=mesh,
        in_specs=(P(("row", "col"), None), P(("row", "col"), None)),
        out_specs=P(("row", "col"), None),
        check_vma=False,
    )
```

profile of v0, /device:TPU:0, one launch (start us, length us, event | category | flops | bytes accessed | tf_op | source)
XLA Modules:
  0.0 151.5 jit_solution(15270870452908466009)
XLA Ops:
  6.5 0.0 all-gather.5.cloned.1.call-start
  6.5 0.7 all-gather.5.cloned.1.call-update
  7.3 0.0 all-gather.3.cloned.1.call-start
  7.3 0.7 all-gather.3.cloned.1.call-update
  8.0 0.0 reduce-scatter.2.cloned.1.call-start
  8.1 11.8 %all_gather.11 = bf16[1024,256]{1,0:T(8,128)(2,1)S(1)} all-gather(bf16[256,256]{1,0:T(8,128)(2,1)} %param.3), channel_id=1, replica_groups=mesh['row'=4,'col'=8] {'row'}, dimensions={0}, use_global_device_ids=true | all-gather | bytes 655360 | tf_op jit(solution)/shard_map/all_gather | solution.py:26
  19.9 27.4 %all-gather.5.cloned.1.call-done = bf16[1024,1024]{1,0:T(8,128)(2,1)} async-done(((bf16[256,1024]{1,0:T(8,128)(2,1)}), bf16[1024,1024]{1,0:T(8,128)(2,1)}) %all-gather.5.cloned.1.call-update) | async-done | bytes 2097168 | tf_op jit(solution)/shard_map/all_gather | solution.py:25
  47.2 0.0 copy-start
  47.2 2.2 %multiply_reduce_fusion.1 = f32[1024]{0:T(1024)S(1)} fusion(bf16[1024,1024]{1,0:T(8,128)(2,1)} %all-gather.5.cloned.1.call-done), kind=kLoop, calls=%fused_computation.3 | loop fusion | flops 3144704 | bytes 2101248 | tf_op jit(solution)/shard_map/reduce_sum | solution.py:10
  49.5 46.6 %all-gather.3.cloned.1.call-done = bf16[2048,1024]{1,0:T(8,128)(2,1)} async-done(((bf16[256,1024]{1,0:T(8,128)(2,1)}), bf16[2048,1024]{1,0:T(8,128)(2,1)}) %all-gather.3.cloned.1.call-update) | async-done | bytes 4194320 | tf_op jit(solution)/shard_map/all_gather | solution.py:29
  96.0 3.1 %multiply_reduce_fusion = f32[2048]{0:T(1024)S(1)} fusion(bf16[2048,1024]{1,0:T(8,128)(2,1)} %all-gather.3.cloned.1.call-done), kind=kLoop, calls=%fused_computation.2 | loop fusion | flops 6289408 | bytes 4202496 | tf_op jit(solution)/shard_map/reduce_sum | solution.py:10
  99.1 0.0 copy-done
  99.1 9.4 %fusion.1 = f32[2048,256]{1,0:T(8,128)} fusion(bf16[1024,256]{1,0:T(8,128)(2,1)S(1)} %all_gather.11, f32[1024]{0:T(1024)S(1)} %multiply_reduce_fusion.1, f32[2048]{0:T(1024)S(1)} %multiply_reduce_fusion, bf16[2048,1024]{1,0:T(8,128)(2,1)} %all-gather.3.cloned.1.call-done, bf16[1024,1024]{1,0:T(8,128)(2,1)S(1)} %copy-done), kind=kOutput, calls=%fused_computation.4 | convolution fusion | flops 5377097728 | bytes 8925184 | tf_op jit(solution)/shard_map/dot_general | solution.py:31
  108.5 0.0 reduce-scatter.2.cloned.1.call-update
  108.5 34.8 %reduce-scatter.2.cloned.1.call-done = f32[256,256]{1,0:T(8,128)} async-done(((f32[2048,256]{1,0:T(8,128)}), f32[256,256]{1,0:T(8,128)}) %reduce-scatter.2.cloned.1.call-update) | async-done | bytes 262160 | tf_op jit(solution)/shard_map/reduce_scatter | solution.py:32
  143.3 1.7 %broadcast_multiply_fusion = f32[256,256]{1,0:T(8,128)} fusion(f32[256,256]{1,0:T(8,128)} %reduce-scatter.2.cloned.1.call-done), kind=kLoop, calls=%fused_computation.5 | loop fusion | flops 65536 | bytes 524288 | tf_op jit(solution)/shard_map/mul | solution.py:33
Async XLA Ops:
  6.5 40.7 %all-gather.5.cloned.1.call-start = ((), (), s32[]{:S(2)}) async-start(), calls=%async_computation.2 | async-start | bytes 2621440 | tf_op jit(solution)/shard_map/all_gather | solution.py:25
  7.3 88.8 %all-gather.3.cloned.1.call-start = ((), (), s32[]{:S(2)}) async-start(), calls=%async_computation.1 | async-start | bytes 4718592 | tf_op jit(solution)/shard_map/all_gather | solution.py:29
  8.0 135.3 %reduce-scatter.2.cloned.1.call-start = ((), (), s32[]{:S(2)}) async-start(), calls=%async_computation.3 | async-start | bytes 2359296 | tf_op jit(solution)/shard_map/reduce_scatter | solution.py:32
  47.2 51.9 %copy-start = (bf16[1024,1024]{1,0:T(8,128)(2,1)S(1)}, bf16[1024,1024]{1,0:T(8,128)(2,1)}, u32[]{:S(2)}) copy-start(bf16[1024,1024]{1,0:T(8,128)(2,1)} %all-gather.5.cloned.1.call-done) | copy-start | bytes 6291460
Sparse Core Ops, SparseCore 0:
  9.2 38.0 all-gather.4
  48.8 47.1 all-gather.2
  108.7 34.5 reduce-scatter.1
where the time goes:
time: 152 us; the launch traced here: 151 us
  waiting for transfers between devices  110 us (72%)
  between operations  13.1 us (9%)
  blocking collectives  11.8 us (8%)
  matrix products  9.4 us (6%)
  other arithmetic  6.96 us (5%)
    all_gather x1, waiting for transfers between devices, per_device(): shard_rows = lax.all_gather(fingerprints, 'col', axis=0, tiled=True)  46.6 us
    reduce_scatter x1, waiting for transfers between devices, per_device(): lax.psum_scatter(partial_value, 'col', scatter_dimension=0, tiled=True)  34.8 us
    all_gather x1, waiting for transfers between devices, per_device(): lax.all_gather(fingerprints, 'row', axis=0, tiled=True)  27.4 us
    all_gather x1, blocking collectives, per_device(): lax.all_gather(probes, 'row', axis=0, tiled=True)  11.8 us
    dot_general x1, matrix products, per_device(): jnp.dot(kernel, column_probes, preferred_element_type=jnp.float32)  9.4 us
    reduce_sum x2, other arithmetic, squares(): return jnp.sum(values * values, axis=1)  5.29 us
  transfers between devices with their start and end apart: 3, of which 3 were waited for; matrix products, arithmetic and copies ran while one was open for 1% of the time, Pallas kernels for 0%

commit v1 on v0

--- a/solution.py
+++ b/solution.py
@@ -26,7 +26,21 @@
         lax.all_gather(probes, "row", axis=0, tiled=True),
     )
     column_sq = squares(column_rows)
-    shard_rows = lax.all_gather(fingerprints, "col", axis=0, tiled=True)
+    ways, here, step = (lax.axis_size("col"), lax.axis_index("col"), fingerprints.shape[0])
+    shape = [n * ways if d == 0 else n for d, n in enumerate(fingerprints.shape)]
+    full = lax.dynamic_update_slice_in_dim(
+        jnp.zeros(shape, fingerprints.dtype), fingerprints, here * step, axis=0
+    )
+    going_up = going_down = fingerprints
+    for far in range(1, ways // 2 + 1):
+        going_up = lax.ppermute(going_up, "col", [(d, (d + 1) % ways) for d in range(ways)])
+        full = lax.dynamic_update_slice_in_dim(full, going_up, (here - far) % ways * step, axis=0)
+        if 2 * far < ways:
+            going_down = lax.ppermute(going_down, "col", [(d, (d - 1) % ways) for d in range(ways)])
+            full = lax.dynamic_update_slice_in_dim(
+                full, going_down, (here + far) % ways * step, axis=0
+            )
+    shard_rows = full
     kernel = tanimoto(shard_rows, column_rows, squares(shard_rows), column_sq)
     partial_value = jnp.dot(kernel, column_probes, preferred_element_type=jnp.float32)
     owned = lax.psum_scatter(partial_value, "col", scatter_dimension=0, tiled=True)

time: 152 us -> 126 us (0.83)
  waiting for transfers between devices: 110 us -> 67.2 us
  starting transfers between devices: 0.08 us -> 10.9 us
  blocking collectives: 11.8 us -> 16.8 us
  local copies, waits for them, and re-layouts: 0.01 us -> 2.81 us
  other arithmetic: 6.96 us -> 4.63 us
    all_gather x1 -> x0, waiting for transfers between devices: 46.6 us -> none  [per_device(): shard_rows = lax.all_gather(fingerprints, 'col', axis=0, tiled=True)]
    ppermute x0 -> x7, waiting for transfers between devices: none -> 32.2 us  [the longest x4 21.4 us: per_device(): lax.ppermute(going_up, 'col', [(d, (d + 1) % ways) for d in range(ways)])]
    all_gather x1, waiting for transfers between devices: 27.4 us -> 0.02 us  [per_device(): lax.all_gather(fingerprints, 'row', axis=0, tiled=True)]
    ppermute x0 -> x7, starting transfers between devices: none -> 10.8 us  [the longest x3 10.3 us: per_device(): lax.ppermute(going_down, 'col', [(d, (d - 1) % ways) for d in range(ways)])]
    all_gather x1, blocking collectives: 11.8 us -> 16.8 us  [per_device(): lax.all_gather(probes, 'row', axis=0, tiled=True)]
    reduce_sum x2, other arithmetic: 5.29 us -> 2.95 us  [squares(): return jnp.sum(values * values, axis=1)]
    unnamed x2 -> x8, local copies, waits for them, and re-layouts: 0.01 us -> 1.94 us
  transfers between devices with their start and end apart: 3 -> 9, of which waited for: 3 -> 6; matrix products, arithmetic and copies ran while one was open for 1% -> 1% of each run, Pallas kernels for 0% -> 0%
where the time goes in v1:
time: 126 us
  waiting for transfers between devices  67.2 us (53%)
  blocking collectives  16.8 us (13%)
  between operations  13.5 us (11%)
  starting transfers between devices  10.9 us (9%)
  matrix products  10.1 us (8%)
  other arithmetic  4.63 us (4%)
  local copies, waits for them, and re-layouts  2.81 us (2%)
    reduce_scatter x1, waiting for transfers between devices, per_device(): lax.psum_scatter(partial_value, 'col', scatter_dimension=0, tiled=True)  34.2 us
    ppermute x4, waiting for transfers between devices, per_device(): lax.ppermute(going_up, 'col', [(d, (d + 1) % ways) for d in range(ways)])  21.4 us
    all_gather x1, blocking collectives, per_device(): lax.all_gather(probes, 'row', axis=0, tiled=True)  16.8 us
    ppermute x3, waiting for transfers between devices, per_device(): lax.ppermute(going_down, 'col', [(d, (d - 1) % ways) for d in range(ways)])  10.8 us
    ppermute x3, starting transfers between devices, per_device(): lax.ppermute(going_down, 'col', [(d, (d - 1) % ways) for d in range(ways)])  10.3 us
    dot_general x1, matrix products, per_device(): jnp.dot(kernel, column_probes, preferred_element_type=jnp.float32)  10.1 us
    reduce_sum x2, other arithmetic, squares(): return jnp.sum(values * values, axis=1)  2.95 us
  transfers between devices with their start and end apart: 9, of which 6 were waited for; matrix products, arithmetic and copies ran while one was open for 1% of the time, Pallas kernels for 0%

profile of v1, /device:TPU:0, one launch (start us, length us, event | category | flops | bytes accessed | tf_op | source)
XLA Modules:
  0.0 125.9 jit_solution(15668860072813294225)
XLA Ops:
  6.5 0.0 copy-start.1
  6.5 0.0 all-gather.2.cloned.1.call-start
  6.5 0.7 all-gather.2.cloned.1.call-update
  7.3 0.0 reduce-scatter.2.cloned.1.call-start
  7.3 0.5 collective-permute-start
  7.8 4.1 %collective-permute-start.1 = (bf16[256,1024]{1,0:T(8,128)(2,1)}, bf16[256,1024]{1,0:T(8,128)(2,1)S(1)}, u32[]{:S(2)}, u32[]{:S(2)}) collective-permute-start(bf16[256,1024]{1,0:T(8,128)(2,1)} %param.2), channel_id=1, source_target_pairs={{0,7},{1,0},{2,1},{3,2},{4,3},{5,4},{6,5},{7,6},{8,15},{9,8},{10,9... | collective-permute-start | bytes 1572872 | tf_op jit(solution)/shard_map/ppermute | solution.py:39
  11.9 10.0 %collective-permute-done = bf16[256,1024]{1,0:T(8,128)(2,1)S(1)} collective-permute-done((bf16[256,1024]{1,0:T(8,128)(2,1)}, bf16[256,1024]{1,0:T(8,128)(2,1)S(1)}, u32[]{:S(2)}, u32[]{:S(2)}) %collective-permute-start) | collective-permute-done | bytes 524320 | tf_op jit(solution)/shard_map/ppermute | solution.py:36
  21.9 0.0 copy-start.2
  21.9 0.0 collective-permute-start.2
  21.9 0.6 collective-permute-done.1
  22.5 3.7 %collective-permute-start.3 = (bf16[256,1024]{1,0:T(8,128)(2,1)S(1)}, bf16[256,1024]{1,0:T(8,128)(2,1)S(1)}, u32[]{:S(2)}, u32[]{:S(2)}) collective-permute-start(bf16[256,1024]{1,0:T(8,128)(2,1)S(1)} %collective-permute-done.1), channel_id=1, source_target_pairs={{0,7},{1,0},{2,1},{3,2},{4,3},{5,4},{6,5},{7,6},{8,15},{9,8},{10,9... | collective-permute-start | bytes 1572872 | tf_op jit(solution)/shard_map/ppermute | solution.py:39
  26.2 8.2 %collective-permute-done.2 = bf16[256,1024]{1,0:T(8,128)(2,1)S(1)} collective-permute-done((bf16[256,1024]{1,0:T(8,128)(2,1)S(1)}, bf16[256,1024]{1,0:T(8,128)(2,1)S(1)}, u32[]{:S(2)}, u32[]{:S(2)}) %collective-permute-start.2) | collective-permute-done | bytes 524320 | tf_op jit(solution)/shard_map/ppermute | solution.py:36
  34.4 0.0 collective-permute-start.4
  34.4 0.0 copy-done.2
  34.4 0.0 copy-start.3
  34.4 16.8 %all_gather.7 = bf16[1024,256]{1,0:T(8,128)(2,1)S(1)} all-gather(bf16[256,256]{1,0:T(8,128)(2,1)} %param.3), channel_id=1, replica_groups=mesh['row'=4,'col'=8] {'row'}, dimensions={0}, use_global_device_ids=true | all-gather | bytes 655360 | tf_op jit(solution)/shard_map/all_gather | solution.py:26
  51.1 0.5 broadcast_in_dim.2
  51.7 0.0 copy-done.1
  51.7 0.0 collective-permute-done.3
  51.7 2.5 %collective-permute-start.5 = (bf16[256,1024]{1,0:T(8,128)(2,1)S(1)}, bf16[256,1024]{1,0:T(8,128)(2,1)S(1)}, u32[]{:S(2)}, u32[]{:S(2)}) collective-permute-start(bf16[256,1024]{1,0:T(8,128)(2,1)S(1)} %collective-permute-done.3), channel_id=1, source_target_pairs={{0,7},{1,0},{2,1},{3,2},{4,3},{5,4},{6,5},{7,6},{8,15},{9,8},{10,9... | collective-permute-start | bytes 1572872 | tf_op jit(solution)/shard_map/ppermute | solution.py:39
  54.2 0.0 copy-done.3
  54.2 0.0 collective-permute-done.4
  54.3 0.1 collective-permute-start.6
  54.5 10.2 %collective-permute-done.5 = bf16[256,1024]{1,0:T(8,128)(2,1)S(1)} collective-permute-done((bf16[256,1024]{1,0:T(8,128)(2,1)S(1)}, bf16[256,1024]{1,0:T(8,128)(2,1)S(1)}, u32[]{:S(2)}, u32[]{:S(2)}) %collective-permute-start.5) | collective-permute-done | bytes 524320 | tf_op jit(solution)/shard_map/ppermute | solution.py:39
  64.8 3.3 %collective-permute-done.6 = bf16[256,1024]{1,0:T(8,128)(2,1)S(1)} collective-permute-done((bf16[256,1024]{1,0:T(8,128)(2,1)S(1)}, bf16[256,1024]{1,0:T(8,128)(2,1)S(1)}, u32[]{:S(2)}, u32[]{:S(2)}) %collective-permute-start.6) | collective-permute-done | bytes 524320 | tf_op jit(solution)/shard_map/ppermute | solution.py:36
  68.1 0.0 copy-start
  68.1 1.9 %copy-done = bf16[2048,1024]{1,0:T(8,128)(2,1)} copy-done((bf16[2048,1024]{1,0:T(8,128)(2,1)}, bf16[2048,1024]{1,0:T(8,128)(2,1)S(1)}, u32[]{:S(2)}) %copy-start) | copy-done | bytes 4194328
  70.1 0.9 multiply_reduce_fusion
  70.9 0.0 all-gather.2.cloned.1.call-done
  71.0 2.1 %multiply_reduce_fusion.1 = f32[1024]{0:T(1024)S(1)} fusion(bf16[1024,1024]{1,0:T(8,128)(2,1)} %all-gather.2.cloned.1.call-done), kind=kLoop, calls=%fused_computation.3 | loop fusion | flops 3144704 | bytes 2101248 | tf_op jit(solution)/shard_map/reduce_sum | solution.py:10
  73.0 10.1 %fusion.1 = f32[2048,256]{1,0:T(8,128)} fusion(bf16[1024,256]{1,0:T(8,128)(2,1)S(1)} %all_gather.7, f32[1024]{0:T(1024)S(1)} %multiply_reduce_fusion.1, f32[2048]{0:T(1024)S(1)} %multiply_reduce_fusion, bf16[2048,1024]{1,0:T(8,128)(2,1)} %copy-done, bf16[1024,1024]{1,0:T(8,128)(2,1)} %all-gather.2.cloned.1.call-done), kind=kOutput, calls=%fused_computation.4 | convolution fusion | flops 5377097728 | bytes 8925184 | tf_op jit(solution)/shard_map/dot_general | solution.py:45
  83.2 0.0 reduce-scatter.2.cloned.1.call-update
  83.2 34.2 %reduce-scatter.2.cloned.1.call-done = f32[256,256]{1,0:T(8,128)} async-done(((f32[2048,256]{1,0:T(8,128)}), f32[256,256]{1,0:T(8,128)}) %reduce-scatter.2.cloned.1.call-update) | async-done | bytes 262160 | tf_op jit(solution)/shard_map/reduce_scatter | solution.py:46
  117.4 1.7 %broadcast_multiply_fusion = f32[256,256]{1,0:T(8,128)} fusion(f32[256,256]{1,0:T(8,128)} %reduce-scatter.2.cloned.1.call-done), kind=kLoop, calls=%fused_computation.5 | loop fusion | flops 65536 | bytes 524288 | tf_op jit(solution)/shard_map/mul | solution.py:47
  (8 shorter events, 0.4 us)
Async XLA Ops:
  6.5 45.1 %copy-start.1 = (bf16[256,1024]{1,0:T(8,128)(2,1)S(1)}, bf16[256,1024]{1,0:T(8,128)(2,1)}, u32[]{:S(2)}) copy-start(bf16[256,1024]{1,0:T(8,128)(2,1)} %param.2) | copy-start | bytes 1572868
  6.5 64.4 %all-gather.2.cloned.1.call-start = ((), (), s32[]{:S(2)}) async-start(), calls=%async_computation.1 | async-start | bytes 2621440 | tf_op jit(solution)/shard_map/all_gather | solution.py:25
  7.3 110.1 %reduce-scatter.2.cloned.1.call-start = ((), (), s32[]{:S(2)}) async-start(), calls=%async_computation.2 | async-start | bytes 2359296 | tf_op jit(solution)/shard_map/reduce_scatter | solution.py:46
  7.3 14.6 %collective-permute-start = (bf16[256,1024]{1,0:T(8,128)(2,1)}, bf16[256,1024]{1,0:T(8,128)(2,1)S(1)}, u32[]{:S(2)}, u32[]{:S(2)}) collective-permute-start(bf16[256,1024]{1,0:T(8,128)(2,1)} %param.2), channel_id=1, source_target_pairs={{0,1},{1,2},{2,3},{3,4},{4,5},{5,6},{6,7},{7,0},{8,9},{9,10},{10,1... | collective-permute-start | bytes 1572872 | tf_op jit(solution)/shard_map/ppermute | solution.py:36
  7.8 14.7 %collective-permute-start.1 = (bf16[256,1024]{1,0:T(8,128)(2,1)}, bf16[256,1024]{1,0:T(8,128)(2,1)S(1)}, u32[]{:S(2)}, u32[]{:S(2)}) collective-permute-start(bf16[256,1024]{1,0:T(8,128)(2,1)} %param.2), channel_id=1, source_target_pairs={{0,7},{1,0},{2,1},{3,2},{4,3},{5,4},{6,5},{7,6},{8,15},{9,8},{10,9... | collective-permute-start | bytes 1572872 | tf_op jit(solution)/shard_map/ppermute | solution.py:39
  21.9 12.5 %copy-start.2 = (bf16[256,1024]{1,0:T(8,128)(2,1)}, bf16[256,1024]{1,0:T(8,128)(2,1)S(1)}, u32[]{:S(2)}) copy-start(bf16[256,1024]{1,0:T(8,128)(2,1)S(1)} %collective-permute-done) | copy-start | bytes 1572868
  21.9 12.5 %collective-permute-start.2 = (bf16[256,1024]{1,0:T(8,128)(2,1)S(1)}, bf16[256,1024]{1,0:T(8,128)(2,1)S(1)}, u32[]{:S(2)}, u32[]{:S(2)}) collective-permute-start(bf16[256,1024]{1,0:T(8,128)(2,1)S(1)} %collective-permute-done), channel_id=1, source_target_pairs={{0,1},{1,2},{2,3},{3,4},{4,5},{5,6},{6,7},{7,0},{8,9},{9,10},{10,1... | collective-permute-start | bytes 1572872 | tf_op jit(solution)/shard_map/ppermute | solution.py:36
  22.5 29.2 %collective-permute-start.3 = (bf16[256,1024]{1,0:T(8,128)(2,1)S(1)}, bf16[256,1024]{1,0:T(8,128)(2,1)S(1)}, u32[]{:S(2)}, u32[]{:S(2)}) collective-permute-start(bf16[256,1024]{1,0:T(8,128)(2,1)S(1)} %collective-permute-done.1), channel_id=1, source_target_pairs={{0,7},{1,0},{2,1},{3,2},{4,3},{5,4},{6,5},{7,6},{8,15},{9,8},{10,9... | collective-permute-start | bytes 1572872 | tf_op jit(solution)/shard_map/ppermute | solution.py:39
  34.4 19.9 %collective-permute-start.4 = (bf16[256,1024]{1,0:T(8,128)(2,1)S(1)}, bf16[256,1024]{1,0:T(8,128)(2,1)S(1)}, u32[]{:S(2)}, u32[]{:S(2)}) collective-permute-start(bf16[256,1024]{1,0:T(8,128)(2,1)S(1)} %collective-permute-done.2), channel_id=1, source_target_pairs={{0,1},{1,2},{2,3},{3,4},{4,5},{5,6},{6,7},{7,0},{8,9},{9,10},{10,1... | collective-permute-start | bytes 1572872 | tf_op jit(solution)/shard_map/ppermute | solution.py:36
  34.4 19.8 %copy-start.3 = (bf16[256,1024]{1,0:T(8,128)(2,1)S(1)}, bf16[256,1024]{1,0:T(8,128)(2,1)}, u32[]{:S(2)}) copy-start(bf16[256,1024]{1,0:T(8,128)(2,1)} %copy-done.2) | copy-start | bytes 1572868
  51.7 13.0 %collective-permute-start.5 = (bf16[256,1024]{1,0:T(8,128)(2,1)S(1)}, bf16[256,1024]{1,0:T(8,128)(2,1)S(1)}, u32[]{:S(2)}, u32[]{:S(2)}) collective-permute-start(bf16[256,1024]{1,0:T(8,128)(2,1)S(1)} %collective-permute-done.3), channel_id=1, source_target_pairs={{0,7},{1,0},{2,1},{3,2},{4,3},{5,4},{6,5},{7,6},{8,15},{9,8},{10,9... | collective-permute-start | bytes 1572872 | tf_op jit(solution)/shard_map/ppermute | solution.py:39
  54.3 13.8 %collective-permute-start.6 = (bf16[256,1024]{1,0:T(8,128)(2,1)S(1)}, bf16[256,1024]{1,0:T(8,128)(2,1)S(1)}, u32[]{:S(2)}, u32[]{:S(2)}) collective-permute-start(bf16[256,1024]{1,0:T(8,128)(2,1)S(1)} %collective-permute-done.4), channel_id=1, source_target_pairs={{0,1},{1,2},{2,3},{3,4},{4,5},{5,6},{6,7},{7,0},{8,9},{9,10},{10,1... | collective-permute-start | bytes 1572872 | tf_op jit(solution)/shard_map/ppermute | solution.py:36
  68.1 1.9 %copy-start = (bf16[2048,1024]{1,0:T(8,128)(2,1)}, bf16[2048,1024]{1,0:T(8,128)(2,1)S(1)}, u32[]{:S(2)}) copy-start(bf16[2048,1024]{1,0:T(8,128)(2,1)S(1)} %constant_dynamic-update-slice_fusion) | copy-start | bytes 12582916
Sparse Core Ops, SparseCore 0:
  9.2 42.0 all-gather.1
  83.3 34.0 reduce-scatter.1
